TPU v7x, 32 devices: a whole 2x2x4 slice. The times are simulated.
32 devices in a mesh: dp: 8 (over y, x, core), seq: 4 (over z).
Axes of the slice: x: 2, y: 2, z: 4, core: 2. Of those that a mesh axis runs over, the one named last changes fastest.
Arguments:
- queries: bfloat16 [8, 512, 1536], P('dp', 'seq'), may hold values from -120 to 120
- keys: bfloat16 [8, 512, 1536], P('dp', 'seq'), may hold values from -4.5 to 4.5
- values: bfloat16 [8, 512, 1536], P('dp', 'seq'), may hold values from -6 to 6
- grad_out: bfloat16 [8, 512, 1536], P('dp', 'seq'), may hold values from -6 to 6
- conv_weight: float32 [31, 1536], replicated, may hold values from -2 to 2
- conv_bias: float32 [1536], replicated, may hold values from -4 to 4
- lengths: int32 [8], P('dp'), may hold values from 128 to 512, as said below
Outputs:
- query_grad: bfloat16 [8, 512, 1536], P('dp', 'seq')
- key_grad: bfloat16 [8, 512, 1536], P('dp', 'seq')
- value_grad: bfloat16 [8, 512, 1536], P('dp', 'seq')
- weight_grad: float32 [31, 1536], P(None, 'seq')
- bias_grad: float32 [1536], P('seq')
Inputs may be any that keep to these rules, and one draw needn't show every extreme that they name: `lengths`: each utterance's valid frames are its first ones; in every draw some utterance has all 512 frames valid.
All inputs are finite; a program needn't handle non-finite values.
Results may differ from a plain program's by a relative error of at most 0.024.
Values may be sent and summed in bfloat16 or wider, within the bound.
No kernel may reach another device: no remote copies, remote signals or barrier semaphores. Data moves between devices by JAX's collectives and lax.ppermute only.
A program may use at most 64 MiB of HBM per device.

v0:
```python
import math

import jax
import jax.numpy as jnp
from jax import lax
from jax.sharding import PartitionSpec as P

HEADS = 16
KERNEL = 31


masked_score = -1e30


def padded_2(block, sides, width):
    for axis, dim in sides:
        count = lax.axis_size(axis)
        forward = [(i, i + 1) for i in range(count - 1)]
        backward = [(target, source) for source, target in forward]
        low = lax.ppermute(
            lax.slice_in_dim(block, block.shape[dim] - width, None, axis=dim), axis, forward
        )
        high = lax.ppermute(lax.slice_in_dim(block, 0, width, axis=dim), axis, backward)
        block = jnp.concatenate([low, block, high], axis=dim)
    return block


def probs_block(query_block, key_heads, key_valid, score_scale):
    scores = (
        jnp.einsum("qhd,khd->hqk", query_block, key_heads, preferred_element_type=jnp.float32)
        * score_scale
    )
    scores = jnp.where(key_valid[None, None, :], scores, masked_score)
    row_top = jnp.max(scores, axis=-1, keepdims=True)
    exped = jnp.exp(scores - row_top)
    return exped / jnp.sum(exped, axis=-1, keepdims=True)


def forward_heads(query_heads, key_heads, value_heads, key_valid, block_rows, score_scale):
    seq_len, heads_here, head_dim = query_heads.shape
    blocks = query_heads.reshape(seq_len // block_rows, block_rows, heads_here, head_dim)

    def block_out(query_block):
        probs = probs_block(query_block, key_heads, key_valid, score_scale)
        return jnp.einsum(
            "hqk,khd->qhd",
            probs.astype(jnp.bfloat16),
            value_heads,
            preferred_element_type=jnp.float32,
        )

    return lax.map(block_out, blocks).reshape(seq_len, heads_here, head_dim)


def backward_heads(
    query_heads, key_heads, value_heads, grad_heads, key_valid, block_rows, score_scale
):
    seq_len, heads_here, head_dim = query_heads.shape
    count = seq_len // block_rows
    query_blocks = query_heads.reshape(count, block_rows, heads_here, head_dim)
    grad_blocks = grad_heads.reshape(count, block_rows, heads_here, head_dim)

    def block_step(carry, inputs):
        key_acc, value_acc = carry
        query_block, grad_block = inputs
        probs = probs_block(query_block, key_heads, key_valid, score_scale)
        probs_low = probs.astype(jnp.bfloat16)
        score_grad = jnp.einsum(
            "qhd,khd->hqk", grad_block, value_heads, preferred_element_type=jnp.float32
        )
        row_delta = jnp.sum(probs * score_grad, axis=-1, keepdims=True)
        diff = (probs * (score_grad - row_delta)).astype(jnp.bfloat16)
        query_part = jnp.einsum("hqk,khd->qhd", diff, key_heads, preferred_element_type=jnp.float32)
        query_part = (query_part * score_scale).astype(jnp.bfloat16)
        key_acc = key_acc + jnp.einsum(
            "hqk,qhd->khd", diff, query_block, preferred_element_type=jnp.float32
        )
        value_acc = value_acc + jnp.einsum(
            "hqk,qhd->khd", probs_low, grad_block, preferred_element_type=jnp.float32
        )
        return ((key_acc, value_acc), query_part)

    zeros = jnp.zeros((seq_len, heads_here, head_dim), jnp.float32)
    (key_acc, value_acc), query_parts = lax.scan(
        block_step, (zeros, zeros), (query_blocks, grad_blocks)
    )
    query_out = query_parts.reshape(seq_len, heads_here, head_dim)
    return (query_out, (key_acc * score_scale).astype(jnp.bfloat16), value_acc.astype(jnp.bfloat16))


def conv_forward(padded, weight, bias, count):
    conv_pre = jnp.zeros(padded[:, 0:count].shape, jnp.float32) + bias
    for j in range(KERNEL):
        conv_pre = conv_pre + weight[j] * padded[:, j : j + count]
    return conv_pre


def silu_slope(conv_pre):
    sig = jax.nn.sigmoid(conv_pre)
    return sig * (1.0 + conv_pre * (1.0 - sig))


def weight_terms(pre_grad_f, padded, count):
    return jnp.stack(
        [jnp.sum(pre_grad_f * padded[:, j : j + count], axis=(0, 1)) for j in range(KERNEL)]
    )


def transposed_conv(grad_pad, weight, count):
    rim = KERNEL // 2
    total = jnp.zeros(grad_pad[:, 0:count].shape, jnp.float32)
    for j in range(KERNEL):
        total = total + weight[j] * grad_pad[:, 2 * rim - j : 2 * rim - j + count]
    return total


def on_device(queries, keys, values, grad_out, conv_weight, conv_bias, lengths):
    seq_count = lax.axis_size("seq")
    seq_rank = lax.axis_index("seq")
    utt_count, frames, width = queries.shape
    head_dim = width // HEADS
    seq_len = frames * seq_count
    block_rows = math.gcd(seq_len, 512)
    score_scale = 1.0 / math.sqrt(head_dim)
    rim = KERNEL // 2
    positions = jnp.arange(seq_len, dtype=jnp.int32)
    key_valid = positions[None, :] < lengths[:, None]

    def split_heads(array):
        return array.reshape(utt_count, frames, HEADS, head_dim)

    query_heads, key_heads, value_heads = (
        lax.all_to_all(split_heads(queries), "seq", split_axis=2, concat_axis=1, tiled=True),
        lax.all_to_all(split_heads(keys), "seq", split_axis=2, concat_axis=1, tiled=True),
        lax.all_to_all(split_heads(values), "seq", split_axis=2, concat_axis=1, tiled=True),
    )
    outputs = [
        forward_heads(
            query_heads[0], key_heads[0], value_heads[0], key_valid[0], block_rows, score_scale
        )
    ]
    attended_heads = jnp.stack(outputs) * key_valid[:, :, None, None].astype(jnp.float32)
    attended_heads = attended_heads.astype(jnp.bfloat16)
    local_frames = seq_rank * frames + jnp.arange(frames, dtype=jnp.int32)
    local_valid = (local_frames[None, :] < lengths[:, None]).astype(jnp.float32)
    attended = lax.all_to_all(
        attended_heads, "seq", split_axis=1, concat_axis=2, tiled=True
    ).reshape(utt_count, frames, width)
    padded = padded_2(attended, (("seq", 1),), rim)
    conv_pre = conv_forward(padded, conv_weight, conv_bias, frames)
    pre_grad = (grad_out.astype(jnp.float32) * silu_slope(conv_pre)).astype(jnp.bfloat16)
    pre_grad_f = pre_grad.astype(jnp.float32)
    weight_part = weight_terms(pre_grad_f, padded, frames)
    bias_part = jnp.sum(pre_grad_f, axis=(0, 1))
    weight_share, bias_share = (
        lax.psum_scatter(
            weight_part.astype(jnp.bfloat16), "seq", scatter_dimension=1, tiled=True
        ).astype(jnp.float32),
        lax.psum_scatter(
            bias_part.astype(jnp.bfloat16), "seq", scatter_dimension=0, tiled=True
        ).astype(jnp.float32),
    )
    weight_grad, bias_grad = lax.psum((weight_share, bias_share), "dp")
    grad_pad = padded_2(pre_grad, (("seq", 1),), rim)
    attn_grad = grad_out.astype(jnp.float32) + transposed_conv(grad_pad, conv_weight, frames)
    attn_grad = (attn_grad * local_valid[:, :, None]).astype(jnp.bfloat16)
    grad_heads = lax.all_to_all(
        split_heads(attn_grad), "seq", split_axis=2, concat_axis=1, tiled=True
    )
    results = [
        backward_heads(
            query_heads[0],
            key_heads[0],
            value_heads[0],
            grad_heads[0],
            key_valid[0],
            block_rows,
            score_scale,
        )
    ]
    query_part = jnp.stack([entry[0] for entry in results])
    key_part = jnp.stack([entry[1] for entry in results])
    value_part = jnp.stack([entry[2] for entry in results])
    query_grad, key_grad, value_grad = (
        lax.all_to_all(query_part, "seq", split_axis=1, concat_axis=2, tiled=True),
        lax.all_to_all(key_part, "seq", split_axis=1, concat_axis=2, tiled=True),
        lax.all_to_all(value_part, "seq", split_axis=1, concat_axis=2, tiled=True),
    )
    query_grad = query_grad.reshape(utt_count, frames, width)
    key_grad = key_grad.reshape(utt_count, frames, width)
    value_grad = value_grad.reshape(utt_count, frames, width)
    return (query_grad, key_grad, value_grad, weight_grad, bias_grad)


def solution(mesh):
    return jax.shard_map(
        on_device,
        mesh=mesh,
        in_specs=(
            P("dp", "seq", None),
            P("dp", "seq", None),
            P("dp", "seq", None),
            P("dp", "seq", None),
            P(),
            P(),
            P("dp"),
        ),
        out_specs=(
            P("dp", "seq", None),
            P("dp", "seq", None),
            P("dp", "seq", None),
            P(None, "seq"),
            P("seq"),
        ),
        check_vma=False,
    )
```

profile of v0, /device:TPU:0, one launch (start us, length us, event | category | flops | bytes accessed | tf_op | source)
XLA Modules:
  0.0 252.3 jit_solution(6834494243588795334)
XLA Ops:
  9.1 6.3 %all-to-all-start = ((bf16[1,128,16,96]{1,3,0,2:T(8,128)(2,1)}), bf16[1,128,16,96]{1,3,0,2:T(8,128)(2,1)S(1)}, u32[]{:S(2)}, u32[]{:S(2)}) async-start(bf16[1,128,16,96]{1,3,0,2:T(8,128)(2,1)} %bitcast.2), calls=%async_computation | async-start | bytes 786432 | tf_op jit(solution)/shard_map/all_to_all | solution.py:133
  17.3 9.8 %all-to-all-done = bf16[1,128,16,96]{1,3,0,2:T(8,128)(2,1)S(1)} async-done(((bf16[1,128,16,96]{1,3,0,2:T(8,128)(2,1)}), bf16[1,128,16,96]{1,3,0,2:T(8,128)(2,1)S(1)}, u32[]{:S(2)}, u32[]{:S(2)}) %all-to-all-start) | async-done | bytes 393248 | tf_op jit(solution)/shard_map/all_to_all | solution.py:133
  27.1 3.5 %all-to-all-start.1 = ((bf16[1,128,16,96]{1,3,0,2:T(8,128)(2,1)}), bf16[1,128,16,96]{1,3,0,2:T(8,128)(2,1)S(1)}, u32[]{:S(2)}, u32[]{:S(2)}) async-start(bf16[1,128,16,96]{1,3,0,2:T(8,128)(2,1)} %bitcast.6), calls=%async_computation.1 | async-start | bytes 786432 | tf_op jit(solution)/shard_map/all_to_all | solution.py:134
  32.5 8.9 %all-to-all-done.1 = bf16[1,128,16,96]{1,3,0,2:T(8,128)(2,1)S(1)} async-done(((bf16[1,128,16,96]{1,3,0,2:T(8,128)(2,1)}), bf16[1,128,16,96]{1,3,0,2:T(8,128)(2,1)S(1)}, u32[]{:S(2)}, u32[]{:S(2)}) %all-to-all-start.1) | async-done | bytes 393248 | tf_op jit(solution)/shard_map/all_to_all | solution.py:134
  46.5 8.2 %all-to-all-done.2 = bf16[1,128,16,96]{1,3,0,2:T(8,128)(2,1)S(1)} async-done(((bf16[1,128,16,96]{1,3,0,2:T(8,128)(2,1)}), bf16[1,128,16,96]{1,3,0,2:T(8,128)(2,1)S(1)}, u32[]{:S(2)}, u32[]{:S(2)}) %all-to-all-start.2) | async-done | bytes 393248 | tf_op jit(solution)/shard_map/all_to_all | solution.py:135
  55.2 3.6 %fusion.160 = (f32[4,512]{1,0:T(4,128)S(1)}, f32[4,512,512]{1,2,0:T(8,128)}) fusion(pred[512]{0:T(512)(128)(4,1)S(1)} %get-tuple-element.139, bf16[512,4,96]{0,2,1:T(8,128)(2,1)S(1)} %squeeze.19, bf16[512,4,96]{0,2,1:T(8,128)(2,1)S(1)} %squeeze.20), kind=kOutput, calls=%fused_computation.382 | convolution fusion | flops 205521408 | bytes 4989440 | tf_op jit(solution)/shard_map/while/body/eval_jaxpr/sub | solution.py:35
  62.6 3.5 %all-to-all-start.3 = ((bf16[1,512,4,96]{3,2,0,1:T(4,128)(2,1)}), bf16[1,512,4,96]{3,2,0,1:T(4,128)(2,1)S(1)}, u32[]{:S(2)}, u32[]{:S(2)}) async-start(bf16[1,512,4,96]{3,2,0,1:T(4,128)(2,1)} %copy.73), calls=%async_computation.3 | async-start | bytes 1048576 | tf_op jit(solution)/shard_map/all_to_all | solution.py:146
  66.4 12.2 %all-to-all-done.3 = bf16[1,512,4,96]{3,2,0,1:T(4,128)(2,1)S(1)} async-done(((bf16[1,512,4,96]{3,2,0,1:T(4,128)(2,1)}), bf16[1,512,4,96]{3,2,0,1:T(4,128)(2,1)S(1)}, u32[]{:S(2)}, u32[]{:S(2)}) %all-to-all-start.3) | async-done | bytes 393248 | tf_op jit(solution)/shard_map/all_to_all | solution.py:146
  82.3 4.8 %collective-permute-done = bf16[1,15,1536]{1,2,0:T(8,128)(2,1)S(1)} collective-permute-done((bf16[1,15,1536]{1,2,0:T(8,128)(2,1)S(1)}, bf16[1,15,1536]{1,2,0:T(8,128)(2,1)S(1)}, u32[]{:S(2)}, u32[]{:S(2)}) %collective-permute-start) | collective-permute-done | bytes 46112 | tf_op jit(solution)/shard_map/ppermute | solution.py:20
  87.1 4.1 %collective-permute-done.1 = bf16[1,15,1536]{1,2,0:T(8,128)(2,1)S(1)} collective-permute-done((bf16[1,15,1536]{1,2,0:T(8,128)(2,1)S(1)}, bf16[1,15,1536]{1,2,0:T(8,128)(2,1)S(1)}, u32[]{:S(2)}, u32[]{:S(2)}) %collective-permute-start.1) | collective-permute-done | bytes 46112 | tf_op jit(solution)/shard_map/ppermute | solution.py:23
  91.2 14.6 %fusion.156 = (bf16[1536]{0:T(1024)(128)(2,1)S(1)}, bf16[1,128,1536]{1,2,0:T(8,128)(2,1)S(1)}) fusion(bf16[1,15,1536]{1,2,0:T(8,128)(2,1)S(1)} %collective-permute-done.1, bf16[1,128,1536]{1,2,0:T(8,128)(2,1)S(1)} %bitcast.80, f32[1536]{0:T(1024)S(1)} %get-tuple-element.125, f32[1536]{0:T(1024)S(1)} %get-tuple-element.126, f32[1536]{0:T(1024)S(1)} %get-tuple-element.97, ...), kind=kLoop, calls=%fused_computation.379 | loop fusion | flops 38140416 | bytes 1471488 | tf_op jit(solution)/shard_map/reduce_sum | solution.py:154
  107.3 4.6 %collective-permute-start.3 = (bf16[1,15,1536]{1,2,0:T(8,128)(2,1)S(1)}, bf16[1,15,1536]{1,2,0:T(8,128)(2,1)S(1)}, u32[]{:S(2)}, u32[]{:S(2)}) collective-permute-start(bf16[1,15,1536]{1,2,0:T(8,128)(2,1)S(1)} %get-tuple-element.132), channel_id=1, source_target_pairs={{0,1},{1,2},{2,3},{4,5},{5,6},{6,7},{8,9},{9,10},{10,11},{12,13},{... | collective-permute-start | bytes 138248 | tf_op jit(solution)/shard_map/ppermute | solution.py:20
  111.9 4.5 %collective-permute-done.2 = bf16[1,15,1536]{1,2,0:T(8,128)(2,1)S(1)} collective-permute-done((bf16[1,15,1536]{1,2,0:T(8,128)(2,1)S(1)}, bf16[1,15,1536]{1,2,0:T(8,128)(2,1)S(1)}, u32[]{:S(2)}, u32[]{:S(2)}) %collective-permute-start.2) | collective-permute-done | bytes 46112 | tf_op jit(solution)/shard_map/ppermute | solution.py:23
  117.5 14.0 %fusion.16 = bf16[1,128,1536]{1,2,0:T(8,128)(2,1)} fusion(bf16[1,128,1536]{1,2,0:T(8,128)(2,1)S(1)} %copy.68, bf16[1,128,1536]{1,2,0:T(8,128)(2,1)S(1)} %get-tuple-element.130, bf16[1,15,1536]{1,2,0:T(8,128)(2,1)S(1)} %collective-permute-done.3, bf16[1,15,1536]{1,2,0:T(8,128)(2,1)S(1)} %collective-permute-done.2, f32[128]{0:T(128)S(1)} %compare_convert_fusion, ...), kind=kLoop, calls=%fused_computation.202 | loop fusion | flops 36569088 | bytes 1462784 | tf_op jit(solution)/shard_map/convert_element_type | solution.py:166
  131.6 5.8 %all-to-all-start.4 = ((bf16[1,128,16,96]{1,3,0,2:T(8,128)(2,1)}), bf16[1,128,16,96]{1,3,0,2:T(8,128)(2,1)S(1)}, u32[]{:S(2)}, u32[]{:S(2)}) async-start(bf16[1,128,16,96]{1,3,0,2:T(8,128)(2,1)} %bitcast.19), calls=%async_computation.4 | async-start | bytes 786432 | tf_op jit(solution)/shard_map/all_to_all | solution.py:167
  140.0 3.9 %fusion.78 = (bf16[1536]{0:T(1024)(128)(2,1)S(1)}, bf16[1536]{0:T(1024)(128)(2,1)S(1)}, bf16[1536]{0:T(1024)(128)(2,1)S(1)}, bf16[1536]{0:T(1024)(128)(2,1)S(1)}...) fusion(bf16[1,128,1536]{1,2,0:T(8,128)(2,1)S(1)} %get-tuple-ele, ...), kind=kLoop, calls=%fused_computation.264 | loop fusion | flops 10799616 | bytes 860160 | tf_op jit(solution)/shard_map/reduce_sum | solution.py:105
  154.1 4.1 %all-to-all-start.7 = ((bf16[1,512,4,96]{3,2,0,1:T(4,128)(2,1)}), bf16[1,512,4,96]{3,2,0,1:T(4,128)(2,1)}, u32[]{:S(2)}, u32[]{:S(2)}) async-start(bf16[1,512,4,96]{3,2,0,1:T(4,128)(2,1)} %copy.87), calls=%async_computation.7 | async-start | bytes 1048576 | tf_op jit(solution)/shard_map/all_to_all | solution.py:187
  158.2 4.6 %multiply_convert_fusion = bf16[4,512,512]{1,2,0:T(8,128)(2,1)S(1)} fusion(f32[4,512,512]{1,2,0:T(8,128)} %get-tuple-element.138, f32[4,512]{1,0:T(4,128)S(1)} %get-tuple-element.137, f32[4,512,512]{1,2,0:T(8,128)} %get-tuple-element.136, f32[4,512]{1,0:T(4,128)S(1)} %get-tuple-element.135), kind=kLoop, calls=%fused_computation.33 | loop fusion | flops 4194304 | bytes 10502144 | tf_op jit(solution)/shard_map/while/body/eval_jaxpr/convert_element_type | solution.py:72
  168.6 4.1 %all-to-all-start.5 = ((bf16[1,512,4,96]{3,2,0,1:T(4,128)(2,1)}), bf16[1,512,4,96]{3,2,0,1:T(4,128)(2,1)}, u32[]{:S(2)}, u32[]{:S(2)}) async-start(bf16[1,512,4,96]{3,2,0,1:T(4,128)(2,1)} %copy.79), calls=%async_computation.5 | async-start | bytes 1048576 | tf_op jit(solution)/shard_map/all_to_all | solution.py:185
  183.3 3.5 %all-to-all-start.6 = ((bf16[1,512,4,96]{3,2,0,1:T(4,128)(2,1)}), bf16[1,512,4,96]{3,2,0,1:T(4,128)(2,1)S(1)}, u32[]{:S(2)}, u32[]{:S(2)}) async-start(bf16[1,512,4,96]{3,2,0,1:T(4,128)(2,1)} %copy.83), calls=%async_computation.6 | async-start | bytes 1048576 | tf_op jit(solution)/shard_map/all_to_all | solution.py:186
  187.1 3.9 %fusion.94 = (bf16[1536]{0:T(1024)(128)(2,1)S(1)}, bf16[1536]{0:T(1024)(128)(2,1)S(1)}, bf16[1536]{0:T(1024)(128)(2,1)S(1)}, bf16[1536]{0:T(1024)(128)(2,1)S(1)}...) fusion(bf16[1,128,1536]{1,2,0:T(8,128)(2,1)S(1)} %get-tuple-ele, ...), kind=kLoop, calls=%fused_computation.280 | loop fusion | flops 10799616 | bytes 860160 | tf_op jit(solution)/shard_map/reduce_sum | solution.py:105
  193.8 12.0 %all-reduce = bf16[1536]{0:T(1024)(128)(2,1)S(1)} all-reduce(bf16[1536]{0:T(1024)(128)(2,1)S(1)} %get-tuple-element.129), channel_id=3, replica_groups=mesh['dp'=8,'seq'=4] {'seq'}, use_global_device_ids=true, to_apply=%region_37.38.clone | all-reduce | flops 1536 | bytes 6144
  205.8 8.4 %reduce-scatter.4.cloned.1.call-done = bf16[384,31]{1,0:T(8,128)(2,1)} async-done(((bf16[1536,31]{1,0:T(8,128)(2,1)}), bf16[384,31]{1,0:T(8,128)(2,1)}) %reduce-scatter.4.cloned.1.call-update) | async-done | bytes 23824
  215.2 23.9 %all-reduce.1 = (f32[31,384]{1,0:T(8,128)}, f32[384]{0:T(512)}) all-reduce(bf16[31,384]{1,0:T(8,128)(2,1)S(1)} %copy.102, f32[384]{0:T(512)S(1)} %dynamic-slice_convert_fusion), channel_id=1, replica_groups=mesh['dp'=8,'seq'=4] {'dp'}, use_global_device_ids=true, to_apply=%region_35.36 | all-reduce | flops 12288 | bytes 74496 | tf_op jit(solution)/shard_map/psum | solution.py:163
  (103 shorter events, 59.6 us)
Async XLA Ops:
  9.1 18.0 %all-to-all-start = ((bf16[1,128,16,96]{1,3,0,2:T(8,128)(2,1)}), bf16[1,128,16,96]{1,3,0,2:T(8,128)(2,1)S(1)}, u32[]{:S(2)}, u32[]{:S(2)}) async-start(bf16[1,128,16,96]{1,3,0,2:T(8,128)(2,1)} %bitcast.2), calls=%async_computation | async-start | bytes 786432 | tf_op jit(solution)/shard_map/all_to_all | solution.py:133
  27.1 14.3 %all-to-all-start.1 = ((bf16[1,128,16,96]{1,3,0,2:T(8,128)(2,1)}), bf16[1,128,16,96]{1,3,0,2:T(8,128)(2,1)S(1)}, u32[]{:S(2)}, u32[]{:S(2)}) async-start(bf16[1,128,16,96]{1,3,0,2:T(8,128)(2,1)} %bitcast.6), calls=%async_computation.1 | async-start | bytes 786432 | tf_op jit(solution)/shard_map/all_to_all | solution.py:134
  41.4 13.3 %all-to-all-start.2 = ((bf16[1,128,16,96]{1,3,0,2:T(8,128)(2,1)}), bf16[1,128,16,96]{1,3,0,2:T(8,128)(2,1)S(1)}, u32[]{:S(2)}, u32[]{:S(2)}) async-start(bf16[1,128,16,96]{1,3,0,2:T(8,128)(2,1)} %bitcast.10), calls=%async_computation.2 | async-start | bytes 786432 | tf_op jit(solution)/shard_map/all_to_all | solution.py:135
  46.0 12.8 %copy-start.1 = (bf16[512,4,96]{0,2,1:T(8,128)(2,1)}, bf16[512,4,96]{0,2,1:T(8,128)(2,1)S(1)}, u32[]{:S(2)}) copy-start(bf16[512,4,96]{0,2,1:T(8,128)(2,1)S(1)} %squeeze.19) | copy-start | bytes 1179652
  46.5 12.3 %copy-start.2 = (bf16[512,4,96]{0,2,1:T(8,128)(2,1)}, bf16[512,4,96]{0,2,1:T(8,128)(2,1)S(1)}, u32[]{:S(2)}) copy-start(bf16[512,4,96]{0,2,1:T(8,128)(2,1)S(1)} %squeeze.20) | copy-start | bytes 1179652
  58.8 7.3 %copy-start.5 = (f32[31,1536]{1,0:T(8,128)S(1)}, f32[31,1536]{1,0:T(8,128)}, u32[]{:S(2)}) copy-start(f32[31,1536]{1,0:T(8,128)} %param.11) | copy-start | bytes 571396
  61.5 20.6 %copy-start.4 = (bf16[1,128,1536]{2,1,0:T(8,128)(2,1)S(1)}, bf16[1,128,1536]{2,1,0:T(8,128)(2,1)}, u32[]{:S(2)}) copy-start(bf16[1,128,1536]{2,1,0:T(8,128)(2,1)} %param.10) | copy-start | bytes 1179652
  61.5 29.7 %copy-start.6 = (f32[1536]{0:T(1024)S(1)}, f32[1536]{0:T(1024)}, u32[]{:S(2)}) copy-start(f32[1536]{0:T(1024)} %param.12) | copy-start | bytes 18436
  62.6 16.0 %all-to-all-start.3 = ((bf16[1,512,4,96]{3,2,0,1:T(4,128)(2,1)}), bf16[1,512,4,96]{3,2,0,1:T(4,128)(2,1)S(1)}, u32[]{:S(2)}, u32[]{:S(2)}) async-start(bf16[1,512,4,96]{3,2,0,1:T(4,128)(2,1)} %copy.73), calls=%async_computation.3 | async-start | bytes 1048576 | tf_op jit(solution)/shard_map/all_to_all | solution.py:146
  79.2 7.8 %collective-permute-start = (bf16[1,15,1536]{1,2,0:T(8,128)(2,1)S(1)}, bf16[1,15,1536]{1,2,0:T(8,128)(2,1)S(1)}, u32[]{:S(2)}, u32[]{:S(2)}) collective-permute-start(bf16[1,15,1536]{1,2,0:T(8,128)(2,1)S(1)} %get-tuple-element.133), channel_id=1, source_target_pairs={{0,1},{1,2},{2,3},{4,5},{5,6},{6,7},{8,9},{9,10},{10,11},{12,13},{... | collective-permute-start | bytes 138248 | tf_op jit(solution)/shard_map/ppermute | solution.py:20
  80.5 10.6 %collective-permute-start.1 = (bf16[1,15,1536]{1,2,0:T(8,128)(2,1)S(1)}, bf16[1,15,1536]{1,2,0:T(8,128)(2,1)S(1)}, u32[]{:S(2)}, u32[]{:S(2)}) collective-permute-start(bf16[1,15,1536]{1,2,0:T(8,128)(2,1)S(1)} %get-tuple-element.134), channel_id=1, source_target_pairs={{1,0},{2,1},{3,2},{5,4},{6,5},{7,6},{9,8},{10,9},{11,10},{13,12},{... | collective-permute-start | bytes 138248 | tf_op jit(solution)/shard_map/ppermute | solution.py:23
  106.0 10.4 %collective-permute-start.2 = (bf16[1,15,1536]{1,2,0:T(8,128)(2,1)S(1)}, bf16[1,15,1536]{1,2,0:T(8,128)(2,1)S(1)}, u32[]{:S(2)}, u32[]{:S(2)}) collective-permute-start(bf16[1,15,1536]{1,2,0:T(8,128)(2,1)S(1)} %get-tuple-element.131), channel_id=1, source_target_pairs={{1,0},{2,1},{3,2},{5,4},{6,5},{7,6},{9,8},{10,9},{11,10},{13,12},{... | collective-permute-start | bytes 138248 | tf_op jit(solution)/shard_map/ppermute | solution.py:23
  107.3 10.3 %collective-permute-start.3 = (bf16[1,15,1536]{1,2,0:T(8,128)(2,1)S(1)}, bf16[1,15,1536]{1,2,0:T(8,128)(2,1)S(1)}, u32[]{:S(2)}, u32[]{:S(2)}) collective-permute-start(bf16[1,15,1536]{1,2,0:T(8,128)(2,1)S(1)} %get-tuple-element.132), channel_id=1, source_target_pairs={{0,1},{1,2},{2,3},{4,5},{5,6},{6,7},{8,9},{9,10},{10,11},{12,13},{... | collective-permute-start | bytes 138248 | tf_op jit(solution)/shard_map/ppermute | solution.py:20
  131.6 14.7 %all-to-all-start.4 = ((bf16[1,128,16,96]{1,3,0,2:T(8,128)(2,1)}), bf16[1,128,16,96]{1,3,0,2:T(8,128)(2,1)S(1)}, u32[]{:S(2)}, u32[]{:S(2)}) async-start(bf16[1,128,16,96]{1,3,0,2:T(8,128)(2,1)} %bitcast.19), calls=%async_computation.4 | async-start | bytes 786432 | tf_op jit(solution)/shard_map/all_to_all | solution.py:167
  146.7 3.5 %copy-start = (f32[4,512,512]{1,2,0:T(8,128)S(1)}, f32[4,512,512]{1,2,0:T(8,128)}, u32[]{:S(2)}) copy-start(f32[4,512,512]{1,2,0:T(8,128)} %get-tuple-element.136) | copy-start | bytes 12582916
  154.1 14.5 %all-to-all-start.7 = ((bf16[1,512,4,96]{3,2,0,1:T(4,128)(2,1)}), bf16[1,512,4,96]{3,2,0,1:T(4,128)(2,1)}, u32[]{:S(2)}, u32[]{:S(2)}) async-start(bf16[1,512,4,96]{3,2,0,1:T(4,128)(2,1)} %copy.87), calls=%async_computation.7 | async-start | bytes 1048576 | tf_op jit(solution)/shard_map/all_to_all | solution.py:187
  158.2 4.6 %copy-start.3 = (bf16[512,4,96]{0,2,1:T(8,128)(2,1)S(1)}, bf16[512,4,96]{0,2,1:T(8,128)(2,1)}, u32[]{:S(2)}) copy-start(bf16[512,4,96]{0,2,1:T(8,128)(2,1)} %copy-done.2) | copy-start | bytes 1179652
  168.6 14.8 %all-to-all-start.5 = ((bf16[1,512,4,96]{3,2,0,1:T(4,128)(2,1)}), bf16[1,512,4,96]{3,2,0,1:T(4,128)(2,1)}, u32[]{:S(2)}, u32[]{:S(2)}) async-start(bf16[1,512,4,96]{3,2,0,1:T(4,128)(2,1)} %copy.79), calls=%async_computation.5 | async-start | bytes 1048576 | tf_op jit(solution)/shard_map/all_to_all | solution.py:185
  172.7 19.8 %copy-start.7 = (u32[32]{0:T(128)S(1)}, u32[32]{0:T(128)}, u32[]{:S(2)}) copy-start(u32[32]{0:T(128)} %constant.60) | copy-start | bytes 388
  183.3 60.8 %all-to-all-start.6 = ((bf16[1,512,4,96]{3,2,0,1:T(4,128)(2,1)}), bf16[1,512,4,96]{3,2,0,1:T(4,128)(2,1)S(1)}, u32[]{:S(2)}, u32[]{:S(2)}) async-start(bf16[1,512,4,96]{3,2,0,1:T(4,128)(2,1)} %copy.83), calls=%async_computation.6 | async-start | bytes 1048576 | tf_op jit(solution)/shard_map/all_to_all | solution.py:186
  186.8 27.4 %reduce-scatter.4.cloned.1.call-start = ((), (), s32[]{:S(2)}) async-start(), calls=%async_computation.9 | async-start | bytes 491520
Sparse Core Ops, SparseCore 0:
  192.6 21.5 reduce-scatter.3
where the time goes:
time: 253 us; the launch traced here: 252 us
  waiting for transfers between devices  70 us (28%)
  other arithmetic  46.5 us (18%)
  starting transfers between devices  43 us (17%)
  blocking collectives  35.9 us (14%)
  local copies, waits for them, and re-layouts  25.1 us (10%)
  matrix products  15.9 us (6%)
  between operations  15.9 us (6%)
    psum x1, blocking collectives, on_device(): weight_grad, bias_grad = lax.psum((weight_share, bias_share), 'dp')  23.9 us
    reduce_sum x1, other arithmetic, on_device(): bias_part = jnp.sum(pre_grad_f, axis=(0, 1))  14.6 us
    convert_element_type x1, other arithmetic, on_device(): attn_grad = (attn_grad * local_valid[:, :, None]).astype(jnp.bfloat16)  14 us
    reduce_sum x4, other arithmetic, weight_terms(): jnp.sum(pre_grad_f * padded[:, j:j + count], axis=(0, 1))  13.1 us
    all_to_all x1, waiting for transfers between devices, on_device(): lax.all_to_all(attended_heads, 'seq', split_axis=1, concat_axis=2, tiled=...  12.2 us
    unnamed x1, blocking collectives  12 us
    unnamed x26, local copies, waits for them, and re-layouts  11.6 us
    all_to_all x1, waiting for transfers between devices, on_device(): lax.all_to_all(split_heads(queries), 'seq', split_axis=2, concat_axis=1,...  9.77 us
  transfers between devices with their start and end apart: 13, of which 12 were waited for; matrix products, arithmetic and copies ran while one was open for 16% of the time, Pallas kernels for 0%

commit v1 on v0

v1 whole, which is shorter than its diff:
```python
import functools
import math

import jax
import jax.numpy as jnp
from jax import lax
from jax.experimental import pallas as pl
from jax.experimental.pallas import tpu as pltpu
from jax.sharding import PartitionSpec as P

HEADS = 16
KERNEL = 31
RIM = KERNEL // 2
PAD = 16
masked_score = -1e30


def head_window(head, head_dim, width):
    first = head * head_dim // 128 * 128
    last = min(-(-(head + 1) * head_dim // 128) * 128, width)
    return first, last


def kernel(
    head_dim,
    block,
    length_ref,
    x_ref,
    weight_ref,
    bias_ref,
    out_ref,
    taps_ref,
    q_t,
    k_t,
    v_t,
    a_t,
    probs,
    shifted,
    attn_grad,
    grad_pad,
    key_acc,
    value_acc,
):
    parts, _, frames, width = x_ref.shape
    rows = parts * frames
    heads = width // head_dim
    blocks = rows // block
    scale = 1.0 / math.sqrt(head_dim)
    log_scale = scale * math.log2(math.e)
    length = length_ref[0]
    f32, bf16 = jnp.float32, jnp.bfloat16

    def rows_of(which):
        return x_ref[:, which].reshape(rows, width)

    for part in range(parts):
        at = pl.ds(part * frames, frames)
        q_t[:, at] = x_ref[part, 0].T
        k_t[:, at] = x_ref[part, 1].T
        v_t[:, at] = x_ref[part, 2].T

    def masked_rows(ref, head, cols):
        first, last = head_window(head, head_dim, width)
        low, high = head * head_dim, (head + 1) * head_dim
        pieces = []
        if low > first:
            pieces.append(jnp.zeros((low - first, block), bf16))
        pieces.append(ref[low:high, cols])
        if last > high:
            pieces.append(jnp.zeros((last - high, block), bf16))
        return jnp.concatenate(pieces, axis=0) if len(pieces) > 1 else pieces[0]

    def head_lanes(array, head):
        first, last = head_window(head, head_dim, width)
        low, high = head * head_dim, (head + 1) * head_dim
        if low == first and high == last:
            return array
        lane = first + lax.broadcasted_iota(jnp.int32, array.shape, 1)
        return jnp.where((lane >= low) & (lane < high), array, jnp.zeros_like(array))

    def forward(index, head):
        cols = pl.ds(pl.multiple_of(index * block, block), block)
        first, last = head_window(head, head_dim, width)
        keys = x_ref[:, 1, :, first:last].reshape(rows, last - first)
        scores = jnp.dot(keys, masked_rows(q_t, head, cols), preferred_element_type=f32)
        key_at = lax.broadcasted_iota(jnp.int32, scores.shape, 0)
        scores = jnp.where(key_at < length, scores, masked_score)
        exped = jnp.exp2((scores - jnp.max(scores, axis=0, keepdims=True)) * log_scale)
        found = exped * (1.0 / jnp.sum(exped, axis=0, keepdims=True))
        probs[head, :, cols] = found
        low, high = head * head_dim, (head + 1) * head_dim
        out = jnp.dot(v_t[low:high, :], found.astype(bf16), preferred_element_type=f32)
        frame_at = index * block + lax.broadcasted_iota(jnp.int32, out.shape, 1)
        a_t[low:high, cols] = jnp.where(frame_at < length, out, 0.0).astype(bf16)

    def each_block(body):
        if blocks == 1:
            for head in range(heads):
                body(0, head)
        else:

            def step(index, carry):
                for head in range(heads):
                    body(index, head)
                return carry

            lax.fori_loop(0, blocks, step, 0)

    each_block(forward)

    tall = shifted.shape[1]

    def shift_all(source_rows):
        shifted[0, 0:PAD, :] = jnp.zeros((PAD, width), f32)
        shifted[0, PAD + rows : tall, :] = jnp.zeros((tall - PAD - rows, width), f32)
        for part in range(parts):
            at = part * frames
            shifted[0, PAD + at : PAD + at + frames, :] = source_rows(part)
        for s in range(1, 8):
            shifted[s, 0 : tall - 8, :] = shifted[0, s : tall - 8 + s, :]

    shift_all(lambda part: a_t[:, pl.ds(part * frames, frames)].T.astype(f32))

    chunk = 64
    lanes = [(at, min(at + 128, width)) for at in range(0, width, 128)]

    def filtered(row, low, high, reverse):
        total = None
        for offset in range(1, KERNEL + 1):
            s, a = offset % 8, offset // 8 * 8
            tap = KERNEL - offset if reverse else offset - 1
            term = weight_ref[tap : tap + 1, low:high] * shifted[s, pl.ds(row + a, chunk), low:high]
            total = term if total is None else total + term
        return total

    for low, high in lanes:

        def conv_step(index, carry, low=low, high=high):
            row = pl.multiple_of(index * chunk, chunk)
            conv_pre = filtered(row, low, high, False) + bias_ref[0:1, low:high]
            sig = 1.0 / (1.0 + jnp.exp(-conv_pre))
            part = row // frames
            grad = x_ref[part, 3, pl.ds(pl.multiple_of(row % frames, chunk), chunk), low:high]
            pre = grad.astype(f32) * (sig * (1.0 + conv_pre * (1.0 - sig)))
            pre = pre.astype(bf16).astype(f32)
            grad_pad[pl.ds(row, chunk), low:high] = pre
            new = []
            for offset in range(1, KERNEL + 1):
                s, a = offset % 8, offset // 8 * 8
                term = pre * shifted[s, pl.ds(row + a, chunk), low:high]
                new.append(carry[offset - 1] + jnp.sum(term.reshape(chunk // 8, 8, high - low), axis=0))
            new.append(carry[KERNEL] + jnp.sum(pre.reshape(chunk // 8, 8, high - low), axis=0))
            return tuple(new)

        zero = jnp.zeros((8, high - low), f32)
        sums = lax.fori_loop(0, rows // chunk, conv_step, (zero,) * (KERNEL + 1))
        for tap in range(KERNEL + 1):
            taps_ref[tap : tap + 1, low:high] = jnp.sum(sums[tap], axis=0, keepdims=True)

    shift_all(lambda part: grad_pad[pl.ds(part * frames, frames), :])

    for low, high in lanes:

        def back_step(index, carry, low=low, high=high):
            row = pl.multiple_of(index * chunk, chunk)
            part = row // frames
            grad = x_ref[part, 3, pl.ds(pl.multiple_of(row % frames, chunk), chunk), low:high]
            total = grad.astype(f32) + filtered(row, low, high, True)
            frame_at = row + lax.broadcasted_iota(jnp.int32, total.shape, 0)
            total = jnp.where(frame_at < length, total, 0.0)
            attn_grad[pl.ds(row, chunk), low:high] = total.astype(bf16)
            return carry

        lax.fori_loop(0, rows // chunk, back_step, 0)

    for part in range(parts):
        at = pl.ds(part * frames, frames)
        a_t[:, at] = attn_grad[at, :].T

    key_acc[...] = jnp.zeros_like(key_acc)
    value_acc[...] = jnp.zeros_like(value_acc)

    def backward(index, head):
        cols = pl.ds(pl.multiple_of(index * block, block), block)
        first, last = head_window(head, head_dim, width)
        low, high = head * head_dim, (head + 1) * head_dim
        values = x_ref[:, 2, :, first:last].reshape(rows, last - first)
        score_grad = jnp.dot(values, masked_rows(a_t, head, cols), preferred_element_type=f32)
        found = probs[head, :, cols]
        delta = jnp.sum(found * score_grad, axis=0, keepdims=True)
        diff = (found * (score_grad - delta)).astype(bf16)
        value_acc[:, first:last] += jnp.dot(
            found.astype(bf16),
            head_lanes(attn_grad[cols, first:last], head),
            preferred_element_type=f32,
        )
        per = block // frames
        queries = x_ref[pl.ds(index * per, per), 0, :, first:last].reshape(block, last - first)
        key_acc[:, first:last] += jnp.dot(
            diff, head_lanes(queries, head), preferred_element_type=f32
        )
        query = jnp.dot(k_t[low:high, :], diff, preferred_element_type=f32)
        q_t[low:high, cols] = (query * scale).astype(bf16)

    each_block(backward)

    for part in range(parts):
        at = pl.ds(part * frames, frames)
        out_ref[part, 0] = q_t[:, at].T
        out_ref[part, 1] = (key_acc[at, :] * scale).astype(bf16)
        out_ref[part, 2] = value_acc[at, :].astype(bf16)


def local_work(moved, weight, bias, lengths, head_dim):
    parts, _, frames, width = moved.shape
    rows = parts * frames
    heads = width // head_dim
    block = math.gcd(rows, 512)
    tall = rows + 2 * PAD + 8
    bf16, f32 = jnp.bfloat16, jnp.float32
    whole = pl.BlockSpec(memory_space=pltpu.VMEM)
    return pl.pallas_call(
        functools.partial(kernel, head_dim, block),
        out_shape=(
            jax.ShapeDtypeStruct((parts, 3, frames, width), bf16),
            jax.ShapeDtypeStruct((KERNEL + 1, width), f32),
        ),
        in_specs=[pl.BlockSpec(memory_space=pltpu.SMEM), whole, whole, whole],
        out_specs=(whole, whole),
        scratch_shapes=[
            pltpu.VMEM((width, rows), bf16),
            pltpu.VMEM((width, rows), bf16),
            pltpu.VMEM((width, rows), bf16),
            pltpu.VMEM((width, rows), bf16),
            pltpu.VMEM((heads, rows, rows), f32),
            pltpu.VMEM((8, tall, width), f32),
            pltpu.VMEM((rows, width), bf16),
            pltpu.VMEM((rows, width), f32),
            pltpu.VMEM((rows, width), f32),
            pltpu.VMEM((rows, width), f32),
        ],
        compiler_params=pltpu.CompilerParams(vmem_limit_bytes=56 * 1024 * 1024),
        cost_estimate=pl.CostEstimate(
            flops=12 * heads * rows * rows * head_dim,
            bytes_accessed=14 * rows * width,
            transcendentals=heads * rows * rows,
        ),
    )(lengths, moved, weight, bias)


def on_device(queries, keys, values, grad_out, conv_weight, conv_bias, lengths):
    seq_count = lax.axis_size("seq")
    seq_rank = lax.axis_index("seq")
    utt_count, frames, width = queries.shape
    head_dim = width // HEADS
    share = width // seq_count
    weight = lax.dynamic_slice_in_dim(conv_weight, seq_rank * share, share, axis=1)
    bias = lax.dynamic_slice_in_dim(conv_bias, seq_rank * share, share, axis=0)[None]
    stacked = jnp.stack([queries[0], keys[0], values[0], grad_out[0]])
    stacked = stacked.reshape(4, frames, seq_count, share).transpose(2, 0, 1, 3)
    moved = lax.all_to_all(stacked, "seq", split_axis=0, concat_axis=0, tiled=True)
    grads, taps = local_work(moved, weight, bias, lengths, head_dim)
    taps = lax.psum(taps, "dp")
    back = lax.all_to_all(grads, "seq", split_axis=0, concat_axis=0, tiled=True)
    back = back.transpose(1, 2, 0, 3).reshape(3, 1, frames, width)
    return back[0], back[1], back[2], taps[:KERNEL], taps[KERNEL]


def solution(mesh):
    return jax.shard_map(
        on_device,
        mesh=mesh,
        in_specs=(
            P("dp", "seq", None),
            P("dp", "seq", None),
            P("dp", "seq", None),
            P("dp", "seq", None),
            P(),
            P(),
            P("dp"),
        ),
        out_specs=(
            P("dp", "seq", None),
            P("dp", "seq", None),
            P("dp", "seq", None),
            P(None, "seq"),
            P("seq"),
        ),
        check_vma=False,
    )
```

time: 253 us -> 102 us (0.40)
  other arithmetic: 46.5 us -> 0.2 us
  starting transfers between devices: 43 us -> 9.98 us
  waiting for transfers between devices: 70 us -> 37.7 us
  Pallas kernels: 0 us -> 16.2 us
  matrix products: 15.9 us -> 0 us
  between operations: 15.9 us -> 1.44 us
  local copies, waits for them, and re-layouts: 25.1 us -> 11.9 us
  blocking collectives: 35.9 us -> 24 us
    reduce_sum x5 -> x0, other arithmetic: 27.7 us -> none  [the longest x1 14.6 us: on_device(): bias_part = jnp.sum(pre_grad_f, axis=(0, 1))]
    all_to_all x8 -> x2, starting transfers between devices: 34.3 us -> 9.98 us  [the longest x1 6.32 us: on_device(): lax.all_to_all(stacked, 'seq', split_axis=0, concat_axis=0, tiled=True)]
    convert_element_type x4 -> x0, other arithmetic: 18.7 us -> none  [the longest x1 14 us: on_device(): attn_grad = (attn_grad * local_valid[:, :, None]).astype(jnp.bfloat16)]
    pallas_call x0 -> x1, Pallas kernels: none -> 16.2 us  [local_work(): pl.pallas_call(functools.partial(kernel, head_dim, block), out_shape=(jax...]
    ppermute x4 -> x0, waiting for transfers between devices: 14.6 us -> none  [the longest x2 8.63 us: padded_2(): lax.ppermute(lax.slice_in_dim(block, 0, width, axis=dim), axis, backward)]
    dot_general x5 -> x0, matrix products: 12.3 us -> none  [the longest x1 3.13 us: block_step(): jnp.einsum('hqk,qhd->khd', probs_low, grad_block, preferred_element_type=...]
    unnamed x1 -> x0, blocking collectives: 12 us -> none
    all_to_all x8 -> x2, waiting for transfers between devices: 46.9 us -> 37.7 us  [the longest x1 34.3 us: on_device(): lax.all_to_all(stacked, 'seq', split_axis=0, concat_axis=0, tiled=True)]
  transfers between devices with their start and end apart: 13 -> 2, of which waited for: 12 -> 2; matrix products, arithmetic and copies ran while one was open for 16% -> 3% of each run, Pallas kernels for 0% -> 0%
where the time goes in v1:
time: 102 us; the launch traced here: 101 us
  waiting for transfers between devices  37.7 us (37%)
  blocking collectives  24 us (24%)
  Pallas kernels  16.2 us (16%)
  local copies, waits for them, and re-layouts  11.9 us (12%)
  starting transfers between devices  9.98 us (10%)
  between operations  1.44 us (1%)
    all_to_all x1, waiting for transfers between devices, on_device(): lax.all_to_all(stacked, 'seq', split_axis=0, concat_axis=0, tiled=True)  34.3 us
    psum x1, blocking collectives, on_device(): taps = lax.psum(taps, 'dp')  24 us
    pallas_call x1, Pallas kernels, local_work(): pl.pallas_call(functools.partial(kernel, head_dim, block), out_shape=(jax...  16.2 us
    unnamed x19, local copies, waits for them, and re-layouts  6.92 us
    all_to_all x1, starting transfers between devices, on_device(): lax.all_to_all(stacked, 'seq', split_axis=0, concat_axis=0, tiled=True)  6.32 us
    all_to_all x1, starting transfers between devices, on_device(): back = lax.all_to_all(grads, 'seq', split_axis=0, concat_axis=0, tiled=True)  3.66 us
    all_to_all x1, waiting for transfers between devices, on_device(): back = lax.all_to_all(grads, 'seq', split_axis=0, concat_axis=0, tiled=True)  3.35 us
  transfers between devices with their start and end apart: 2, of which 2 were waited for; matrix products, arithmetic and copies ran while one was open for 3% of the time, Pallas kernels for 0%

profile of v1, /device:TPU:0, one launch (start us, length us, event | category | flops | bytes accessed | tf_op | source)
XLA Modules:
  0.0 101.4 jit_solution(3736271523086129912)
XLA Ops:
  0.7 1.3 %copy.15 = bf16[1,128,1536]{1,2,0:T(8,128)(2,1)S(1)} copy(bf16[1,128,1536]{2,1,0:T(8,128)(2,1)} %param.10) | data formatting | bytes 786432 | tf_op args[3]
  2.0 1.2 %copy.14 = bf16[1,128,1536]{1,2,0:T(8,128)(2,1)S(1)} copy(bf16[1,128,1536]{2,1,0:T(8,128)(2,1)} %param.9) | data formatting | bytes 786432 | tf_op args[2]
  3.2 0.2 copy.13
  3.4 0.2 copy.12
  3.7 0.2 pad_maximum_fusion
  3.9 1.6 %copy.16 = bf16[4,128,4,384]{3,1,0,2:T(8,128)(2,1)} copy(bf16[4,128,4,384]{1,3,2,0:T(8,128)(2,1)S(1)} %bitcast.7) | data formatting | bytes 3145728 | tf_op jit(solution)/shard_map/reshape | solution.py:260
  5.5 6.3 %all-to-all-start = ((bf16[4,4,128,384]{3,2,1,0:T(8,128)(2,1)}), bf16[4,4,128,384]{3,2,1,0:T(8,128)(2,1)S(1)}, u32[]{:S(2)}, u32[]{:S(2)}) async-start(bf16[4,4,128,384]{3,2,1,0:T(8,128)(2,1)} %bitcast.1), calls=%async_computation | async-start | bytes 3145728 | tf_op jit(solution)/shard_map/all_to_all | solution.py:261
  12.4 0.8 dynamic_slice.7
  13.2 0.6 broadcast_in_dim.3.bias_ref
  13.8 0.6 constant_dynamic-slice_fusion.weight_ref
  14.4 34.3 %all-to-all-done.x_ref = bf16[4,4,128,384]{3,2,1,0:T(8,128)(2,1)S(1)} async-done(((bf16[4,4,128,384]{3,2,1,0:T(8,128)(2,1)}), bf16[4,4,128,384]{3,2,1,0:T(8,128)(2,1)S(1)}, u32[]{:S(2)}, u32[]{:S(2)}) %all-to-all-start) | async-done | bytes 1572896 | tf_op jit(solution)/shard_map/all_to_all | solution.py:261
  48.7 1.2 %copy-done.1 = bf16[4,4,128,384]{3,2,1,0:T(8,128)(2,1)} copy-done((bf16[4,4,128,384]{3,2,1,0:T(8,128)(2,1)}, bf16[4,4,128,384]{3,2,1,0:T(8,128)(2,1)S(1)}, u32[]{:S(2)}) %copy-start.1) | copy-done | bytes 1572888
  49.9 16.2 %shard_map.110 = (bf16[4,3,128,384]{3,2,1,0:T(8,128)(2,1)}, f32[32,384]{1,0:T(8,128)}) custom-call(s32[1]{0:T(128)S(6)} %copy.23.length_ref, bf16[4,4,128,384]{3,2,1,0:T(8,128)(2,1)} %copy-done.1, f32[31,384]{1,0:T(8,128)} %constant_dynamic-slice_fusion.weight_ref, f32[1,384]{1,0:T(1,128)} %broadcast_in_dim.3.bias_ref), custom_call_target="tpu_custom_call" | custom-call | flops 1207959552 | bytes 2752512 | tf_op jit(solution)/shard_map/pallas_call | solution.py:222
  66.1 3.7 %all-to-all-start.1 = ((bf16[4,3,128,384]{3,2,1,0:T(8,128)(2,1)}), bf16[4,3,128,384]{3,2,1,0:T(8,128)(2,1)S(1)}, u32[]{:S(2)}, u32[]{:S(2)}) async-start(bf16[4,3,128,384]{3,2,1,0:T(8,128)(2,1)} %get-tuple-element.7), calls=%async_computation.1 | async-start | bytes 2359296 | tf_op jit(solution)/shard_map/all_to_all | solution.py:264
  69.8 24.0 %psum.7 = f32[32,384]{1,0:T(8,128)S(1)} all-reduce(f32[32,384]{1,0:T(8,128)S(1)} %copy-done.5), channel_id=1, replica_groups=mesh['dp'=8,'seq'=4] {'dp'}, use_global_device_ids=true, to_apply=%region_0.0 | all-reduce | flops 12288 | bytes 98304 | tf_op jit(solution)/shard_map/psum | solution.py:263
  93.8 0.6 slice_reduce_fusion
  94.4 3.3 %all-to-all-done.1 = bf16[4,3,128,384]{3,2,1,0:T(8,128)(2,1)S(1)} async-done(((bf16[4,3,128,384]{3,2,1,0:T(8,128)(2,1)}), bf16[4,3,128,384]{3,2,1,0:T(8,128)(2,1)S(1)}, u32[]{:S(2)}, u32[]{:S(2)}) %all-to-all-start.1) | async-done | bytes 1179680 | tf_op jit(solution)/shard_map/all_to_all | solution.py:264
  97.8 0.1 fusion
  97.9 0.2 copy.17
  98.2 0.9 copy.20
  99.1 0.2 copy.18
  99.3 0.9 copy.21
  100.3 0.2 copy.19
  100.5 0.9 copy.22
  (11 shorter events, 0.0 us)
Async XLA Ops:
  0.6 13.1 %copy-start = (f32[31,1536]{1,0:T(8,128)S(1)}, f32[31,1536]{1,0:T(8,128)}, u32[]{:S(2)}) copy-start(f32[31,1536]{1,0:T(8,128)} %param.11) | copy-start | bytes 571396
  0.6 2.5 %copy-start.2 = (bf16[1,128,1536]{2,1,0:T(8,128)(2,1)S(1)}, bf16[1,128,1536]{2,1,0:T(8,128)(2,1)}, u32[]{:S(2)}) copy-start(bf16[1,128,1536]{2,1,0:T(8,128)(2,1)} %param.8) | copy-start | bytes 1179652
  0.7 2.8 %copy-start.3 = (bf16[1,128,1536]{2,1,0:T(8,128)(2,1)S(1)}, bf16[1,128,1536]{2,1,0:T(8,128)(2,1)}, u32[]{:S(2)}) copy-start(bf16[1,128,1536]{2,1,0:T(8,128)(2,1)} %param.7) | copy-start | bytes 1179652
  5.5 43.3 %all-to-all-start = ((bf16[4,4,128,384]{3,2,1,0:T(8,128)(2,1)}), bf16[4,4,128,384]{3,2,1,0:T(8,128)(2,1)S(1)}, u32[]{:S(2)}, u32[]{:S(2)}) async-start(bf16[4,4,128,384]{3,2,1,0:T(8,128)(2,1)} %bitcast.1), calls=%async_computation | async-start | bytes 3145728 | tf_op jit(solution)/shard_map/all_to_all | solution.py:261
  48.7 1.2 %copy-start.1 = (bf16[4,4,128,384]{3,2,1,0:T(8,128)(2,1)}, bf16[4,4,128,384]{3,2,1,0:T(8,128)(2,1)S(1)}, u32[]{:S(2)}) copy-start(bf16[4,4,128,384]{3,2,1,0:T(8,128)(2,1)S(1)} %all-to-all-done.x_ref) | copy-start | bytes 4718596
  66.1 3.7 %copy-start.5 = (f32[32,384]{1,0:T(8,128)S(1)}, f32[32,384]{1,0:T(8,128)}, u32[]{:S(2)}) copy-start(f32[32,384]{1,0:T(8,128)} %get-tuple-element.8) | copy-start | bytes 147460
  66.1 31.7 %all-to-all-start.1 = ((bf16[4,3,128,384]{3,2,1,0:T(8,128)(2,1)}), bf16[4,3,128,384]{3,2,1,0:T(8,128)(2,1)S(1)}, u32[]{:S(2)}, u32[]{:S(2)}) async-start(bf16[4,3,128,384]{3,2,1,0:T(8,128)(2,1)} %get-tuple-element.7), calls=%async_computation.1 | async-start | bytes 2359296 | tf_op jit(solution)/shard_map/all_to_all | solution.py:264
  93.8 4.3 %copy-start.4 = (f32[32,384]{1,0:T(8,128)}, f32[32,384]{1,0:T(8,128)S(1)}, u32[]{:S(2)}) copy-start(f32[32,384]{1,0:T(8,128)S(1)} %psum.7) | copy-start | bytes 147460
